TPU v7x, 32 devices: a whole 2x2x4 slice. The times are simulated.
32 devices in a mesh: dp: 8 (over z, x), mp: 4 (over y, core).
Axes of the slice: x: 2, y: 2, z: 4, core: 2. Of those that a mesh axis runs over, the one named last changes fastest.
Arguments:
- tokens: bfloat16 [8192, 768], P('dp'), may hold values from -6 to 6
- memory: bfloat16 [8192, 768], P('dp'), may hold values from -6 to 6
- cotangent: bfloat16 [8192, 768], P('dp'), may hold values from -6 to 6
- table_lengths: int32 [8, 4], P('dp'), may hold values from 1 to 512, 1024 in all within a row
- table_plots: int32 [8, 4], P('dp'), may hold values from 0 to 3, each once within a row
- gains: float32 [768, 3], replicated, may hold values from 0.5 to 1.5
- w_qkv: bfloat16 [768, 3, 768], P(None, None, 'mp'), may hold values from -0.21875 to 0.21875
- w_self_out: bfloat16 [768, 768], P(None, 'mp'), may hold values from -0.625 to 0.625
- w_cross_query: bfloat16 [768, 768], P(None, 'mp'), may hold values from -0.21875 to 0.21875
- w_cross_kv: bfloat16 [768, 2, 768], P(None, None, 'mp'), may hold values from -0.21875 to 0.21875
- w_cross_out: bfloat16 [768, 768], P(None, 'mp'), may hold values from -0.875 to 0.875
- w_gate_up: bfloat16 [768, 2, 2048], P(None, None, 'mp'), may hold values from -0.21875 to 0.21875
- w_down: bfloat16 [768, 2048], P(None, 'mp'), may hold values from -0.125 to 0.125
Outputs:
- layer_out: bfloat16 [8192, 768], P('dp')
- grad_tokens: float32 [8192, 768], P('dp')
- grad_memory: float32 [8192, 768], P('dp')
- grad_gains: float32 [768, 3], P('dp')
- grad_qkv: float32 [768, 3, 768], P('dp', None, 'mp')
- grad_self_out: float32 [768, 768], P('dp', 'mp')
- grad_cross_query: float32 [768, 768], P('dp', 'mp')
- grad_cross_kv: float32 [768, 2, 768], P('dp', None, 'mp')
- grad_cross_out: float32 [768, 768], P('dp', 'mp')
- grad_gate_up: float32 [768, 2, 2048], P('dp', None, 'mp')
- grad_down: float32 [768, 2048], P('dp', 'mp')
- step_qkv: float32 [768, 3, 768], P('dp', None, 'mp')
- step_self_out: float32 [768, 768], P('dp', 'mp')
- step_cross_query: float32 [768, 768], P('dp', 'mp')
- step_cross_kv: float32 [768, 2, 768], P('dp', None, 'mp')
- step_cross_out: float32 [768, 768], P('dp', 'mp')
- step_gate_up: float32 [768, 2, 2048], P('dp', None, 'mp')
- step_down: float32 [768, 2048], P('dp', 'mp')
Inputs may be any that keep to these rules, and one draw needn't show every extreme that they name: `table_lengths`: each pack's 4 lengths add up to 1024, and the longest is 512. `table_plots`: each pack's row is a permutation of its 4 plots.
All inputs are finite; a program needn't handle non-finite values.
Results may differ from a plain program's by a relative error of at most 0.02.
Values sent between devices are 32-bit elements; how exact they have to be, the bound alone decides.
No kernel may reach another device: no remote copies, remote signals or barrier semaphores. Data moves between devices by JAX's collectives and lax.ppermute only.
A program may use at most 128 MiB of HBM per device.

v0:
```python
import math

import jax
import jax.numpy as jnp
from jax import lax
from jax.sharding import PartitionSpec as P

DH = 64
PATCH = 256


def norm_apply(hidden_in, gain_col):
    return (
        hidden_in
        * lax.rsqrt(jnp.mean(hidden_in * hidden_in, axis=-1, keepdims=True) + 1e-06)
        * gain_col
    )


def table_ids(length_row, plot_row, slot_count):
    ends = jnp.cumsum(length_row)
    places = jnp.arange(slot_count, dtype=jnp.int32)
    segment = jnp.sum((places[:, None] >= ends[None, :]).astype(jnp.int32), axis=1)
    tables = jnp.arange(length_row.shape[0], dtype=jnp.int32)
    chosen = (segment[:, None] == tables[None, :]).astype(jnp.int32)
    plot_of = jnp.sum(chosen * plot_row[None, :], axis=1)
    return (segment, plot_of)


def probs_of(query, keys, allowed, score_scale):
    raw = jnp.einsum("qhd,khd->hqk", query, keys, preferred_element_type=jnp.float32) * score_scale
    masked = jnp.where(allowed[None], raw, -1e30)
    highest = jnp.max(masked, axis=-1, keepdims=True)
    expd = jnp.exp(masked - highest)
    return expd / jnp.sum(expd, axis=-1, keepdims=True)


def attend_forward(query, keys, values, allowed, score_scale):
    probs = probs_of(query, keys, allowed, score_scale).astype(jnp.bfloat16)
    mixed = jnp.einsum("hqk,khd->qhd", probs, values, preferred_element_type=jnp.float32)
    return mixed.astype(jnp.bfloat16)


def attend_backward(query, keys, values, allowed, score_scale, grad_mixed):
    probs = probs_of(query, keys, allowed, score_scale)
    low_probs = probs.astype(jnp.bfloat16)
    grad_values = jnp.einsum(
        "hqk,qhd->khd", low_probs, grad_mixed, preferred_element_type=jnp.float32
    )
    grad_probs = jnp.einsum("qhd,khd->hqk", grad_mixed, values, preferred_element_type=jnp.float32)
    inner = jnp.sum(probs * grad_probs, axis=-1, keepdims=True)
    grad_scores = (probs * (grad_probs - inner)).astype(jnp.bfloat16)
    grad_query = (
        jnp.einsum("hqk,khd->qhd", grad_scores, keys, preferred_element_type=jnp.float32)
        * score_scale
    )
    grad_keys = (
        jnp.einsum("hqk,qhd->khd", grad_scores, query, preferred_element_type=jnp.float32)
        * score_scale
    )
    return (
        grad_query.astype(jnp.bfloat16),
        grad_keys.astype(jnp.bfloat16),
        grad_values.astype(jnp.bfloat16),
    )


def project_out(mixed_flat, weight):
    return jnp.einsum("sc,dc->sd", mixed_flat, weight, preferred_element_type=jnp.float32)


def branch_total(partial_out):
    return lax.psum(partial_out, "mp")


def input_total(partial_grad):
    return lax.psum(partial_grad, "mp")


def scaled_update(flat_rows, row_mean, col_mean, mean_rows, shape_out):
    factor = row_mean[:, None] * col_mean[None, :] / mean_rows
    return (flat_rows * lax.rsqrt(factor)).reshape(shape_out)


def adafactor_sharded(shards, model_width):
    flats = tuple((piece.reshape(piece.shape[0], -1) for piece in shards))
    row_local = tuple((jnp.sum(matrix * matrix, axis=1) for matrix in flats))
    row_sums = lax.psum(row_local, "mp")
    row_means = tuple(
        (
            total / (matrix.shape[1] * lax.axis_size("mp")) + 1e-30
            for total, matrix in zip(row_sums, flats)
        )
    )
    col_local = tuple((jnp.sum(matrix * matrix, axis=0) for matrix in flats))
    mean_local = tuple((jnp.sum(means) for means in row_means))
    summed = lax.psum(col_local + mean_local, "dp")
    count = len(flats)
    results = []
    for index_mat in range(count):
        col_mean = summed[index_mat] / model_width + 1e-30
        mean_rows = summed[count + index_mat] / model_width
        results.append(
            scaled_update(
                flats[index_mat], row_means[index_mat], col_mean, mean_rows, shards[index_mat].shape
            )
        )
    return tuple(results)


def on_device(
    tokens,
    memory,
    cotangent,
    table_lengths,
    table_plots,
    gains,
    w_qkv,
    w_self_out,
    w_cross_query,
    w_cross_kv,
    w_cross_out,
    w_gate_up,
    w_down,
):
    slot_count, model_width = tokens.shape
    mem_count = memory.shape[0]
    heads_here = w_self_out.shape[1] // DH
    units_here = w_down.shape[1]
    score_scale = 1.0 / math.sqrt(DH)
    segment, plot_of = table_ids(table_lengths[0], table_plots[0], slot_count)
    places = jnp.arange(slot_count, dtype=jnp.int32)
    self_mask = (segment[:, None] == segment[None, :]) & (places[None, :] <= places[:, None])
    key_plot = jnp.arange(mem_count, dtype=jnp.int32) // PATCH
    cross_mask = plot_of[:, None] == key_plot[None, :]
    inputs = tokens.astype(jnp.float32)
    normed_a = norm_apply(inputs, gains[:, 0]).astype(jnp.bfloat16)
    qkv = jnp.dot(normed_a, w_qkv.reshape(model_width, -1), preferred_element_type=jnp.float32)
    qkv = qkv.astype(jnp.bfloat16).reshape(slot_count, 3, heads_here, DH)
    mixed_a = attend_forward(qkv[:, 0], qkv[:, 1], qkv[:, 2], self_mask, score_scale)
    flat_a = mixed_a.reshape(slot_count, -1)
    first = inputs + branch_total(project_out(flat_a, w_self_out))
    normed_b = norm_apply(first, gains[:, 1]).astype(jnp.bfloat16)
    query_b = jnp.dot(normed_b, w_cross_query, preferred_element_type=jnp.float32).astype(
        jnp.bfloat16
    )
    query_b = query_b.reshape(slot_count, heads_here, DH)
    kv_b = jnp.dot(memory, w_cross_kv.reshape(model_width, -1), preferred_element_type=jnp.float32)
    kv_b = kv_b.astype(jnp.bfloat16).reshape(mem_count, 2, heads_here, DH)
    mixed_b = attend_forward(query_b, kv_b[:, 0], kv_b[:, 1], cross_mask, score_scale)
    flat_b = mixed_b.reshape(slot_count, -1)
    second = first + branch_total(project_out(flat_b, w_cross_out))
    normed_c = norm_apply(second, gains[:, 2]).astype(jnp.bfloat16)
    gate_up = jnp.dot(
        normed_c, w_gate_up.reshape(model_width, -1), preferred_element_type=jnp.float32
    )
    gate_up = gate_up.reshape(slot_count, 2, units_here)

    def gated(gate_in, up_in):
        return jax.nn.gelu(gate_in, approximate=True) * up_in

    hidden = gated(gate_up[:, 0], gate_up[:, 1]).astype(jnp.bfloat16)
    result = second + branch_total(
        jnp.einsum("sf,df->sd", hidden, w_down, preferred_element_type=jnp.float32)
    )
    layer_out = result.astype(jnp.bfloat16)
    grad_result = cotangent.astype(jnp.float32)
    grad_w_down = jnp.einsum("sd,sf->df", cotangent, hidden, preferred_element_type=jnp.float32)
    grad_hidden = jnp.dot(cotangent, w_down, preferred_element_type=jnp.float32)
    unused_value, pull_gate = jax.vjp(gated, gate_up[:, 0], gate_up[:, 1])
    grad_gate, grad_up = pull_gate(grad_hidden)
    grad_gu = jnp.stack([grad_gate, grad_up], axis=1).astype(jnp.bfloat16)
    grad_w_gate_up = jnp.einsum(
        "sd,skf->dkf", normed_c, grad_gu, preferred_element_type=jnp.float32
    )
    grad_normed_c = input_total(
        jnp.einsum("skf,dkf->sd", grad_gu, w_gate_up, preferred_element_type=jnp.float32)
    )
    unused_value, pull_norm_c = jax.vjp(norm_apply, second, gains[:, 2])
    grad_second_norm, grad_gain_c = pull_norm_c(grad_normed_c)
    grad_second = grad_result + grad_second_norm
    branch_grad_b = grad_second.astype(jnp.bfloat16)
    grad_w_cross_out = jnp.einsum(
        "sd,sc->dc", branch_grad_b, flat_b, preferred_element_type=jnp.float32
    )
    grad_mixed_b = jnp.dot(branch_grad_b, w_cross_out, preferred_element_type=jnp.float32).astype(
        jnp.bfloat16
    )
    grad_mixed_b = grad_mixed_b.reshape(slot_count, heads_here, DH)
    grad_query_b, grad_keys_b, grad_values_b = attend_backward(
        query_b, kv_b[:, 0], kv_b[:, 1], cross_mask, score_scale, grad_mixed_b
    )
    grad_query_flat = grad_query_b.reshape(slot_count, -1)
    grad_kv = jnp.stack([grad_keys_b, grad_values_b], axis=1).reshape(mem_count, 2, -1)
    grad_w_cross_query = jnp.einsum(
        "sd,sc->dc", normed_b, grad_query_flat, preferred_element_type=jnp.float32
    )
    grad_w_cross_kv = jnp.einsum("md,mkc->dkc", memory, grad_kv, preferred_element_type=jnp.float32)
    part_normed = jnp.einsum(
        "sc,dc->sd", grad_query_flat, w_cross_query, preferred_element_type=jnp.float32
    )
    part_memory = jnp.einsum("mkc,dkc->md", grad_kv, w_cross_kv, preferred_element_type=jnp.float32)
    grad_normed_b, grad_memory = lax.psum((part_normed, part_memory), "mp")
    unused_value, pull_norm_b = jax.vjp(norm_apply, first, gains[:, 1])
    grad_first_norm, grad_gain_b = pull_norm_b(grad_normed_b)
    grad_first = grad_second + grad_first_norm
    branch_grad_a = grad_first.astype(jnp.bfloat16)
    grad_w_self_out = jnp.einsum(
        "sd,sc->dc", branch_grad_a, flat_a, preferred_element_type=jnp.float32
    )
    grad_mixed_a = jnp.dot(branch_grad_a, w_self_out, preferred_element_type=jnp.float32).astype(
        jnp.bfloat16
    )
    grad_mixed_a = grad_mixed_a.reshape(slot_count, heads_here, DH)
    grad_query_a, grad_keys_a, grad_values_a = attend_backward(
        qkv[:, 0], qkv[:, 1], qkv[:, 2], self_mask, score_scale, grad_mixed_a
    )
    grad_qkv_rows = jnp.stack([grad_query_a, grad_keys_a, grad_values_a], axis=1).reshape(
        slot_count, 3, -1
    )
    grad_w_qkv = jnp.einsum(
        "sd,skc->dkc", normed_a, grad_qkv_rows, preferred_element_type=jnp.float32
    )
    grad_normed_a = input_total(
        jnp.einsum("skc,dkc->sd", grad_qkv_rows, w_qkv, preferred_element_type=jnp.float32)
    )
    unused_value, pull_norm_a = jax.vjp(norm_apply, inputs, gains[:, 0])
    grad_input_norm, grad_gain_a = pull_norm_a(grad_normed_a)
    grad_tokens = grad_first + grad_input_norm
    grad_gain_all = jnp.stack([grad_gain_a, grad_gain_b, grad_gain_c], axis=1)
    partials = (
        grad_gain_all,
        grad_w_qkv,
        grad_w_self_out,
        grad_w_cross_query,
        grad_w_cross_kv,
        grad_w_cross_out,
        grad_w_gate_up,
        grad_w_down,
    )
    shards = (
        lax.psum_scatter(partials[0], "dp", scatter_dimension=0, tiled=True),
        lax.psum_scatter(partials[1], "dp", scatter_dimension=0, tiled=True),
        lax.psum_scatter(partials[2], "dp", scatter_dimension=0, tiled=True),
        lax.psum_scatter(partials[3], "dp", scatter_dimension=0, tiled=True),
        lax.psum_scatter(partials[4], "dp", scatter_dimension=0, tiled=True),
        lax.psum_scatter(partials[5], "dp", scatter_dimension=0, tiled=True),
        lax.psum_scatter(partials[6], "dp", scatter_dimension=0, tiled=True),
        lax.psum_scatter(partials[7], "dp", scatter_dimension=0, tiled=True),
    )
    updates = adafactor_sharded(shards[1:], model_width)
    return (
        layer_out,
        grad_tokens,
        grad_memory,
        shards[0],
        shards[1],
        shards[2],
        shards[3],
        shards[4],
        shards[5],
        shards[6],
        shards[7],
        updates[0],
        updates[1],
        updates[2],
        updates[3],
        updates[4],
        updates[5],
        updates[6],
    )


def solution(mesh):
    placed = (
        P("dp", None),
        P("dp", None),
        P("dp", None),
        P("dp", None),
        P("dp", None),
        P(),
        P(None, None, "mp"),
        P(None, "mp"),
        P(None, "mp"),
        P(None, None, "mp"),
        P(None, "mp"),
        P(None, None, "mp"),
        P(None, "mp"),
    )
    return jax.shard_map(
        on_device,
        mesh=mesh,
        in_specs=placed,
        out_specs=(
            P("dp", None),
            P("dp", None),
            P("dp", None),
            P("dp", None),
            P("dp", None, "mp"),
            P("dp", "mp"),
            P("dp", "mp"),
            P("dp", None, "mp"),
            P("dp", "mp"),
            P("dp", None, "mp"),
            P("dp", "mp"),
            P("dp", None, "mp"),
            P("dp", "mp"),
            P("dp", "mp"),
            P("dp", None, "mp"),
            P("dp", "mp"),
            P("dp", None, "mp"),
            P("dp", "mp"),
        ),
        check_vma=False,
    )
```

profile of v0, /device:TPU:0, one launch (start us, length us, event | category | flops | bytes accessed | tf_op | source)
XLA Modules:
  0.0 1114.6 jit_solution(2685970286471968532)
XLA Ops:
  15.9 10.4 fusion.103
  26.3 6.0 fusion.50
  39.7 66.2 %all-reduce.9.cloned.1.call-done = f32[1024,768]{1,0:T(8,128)} async-done(((f32[1024,768]{1,0:T(8,128)}), f32[1024,768]{1,0:T(8,128)}) %all-reduce.9.cloned.1.call-update) | async-done | bytes 3145744 | tf_op jit(solution)/shard_map/psum | solution.py:73
  110.8 10.3 fusion.104
  121.1 6.0 fusion.56
  133.8 65.1 %all-reduce.11.cloned.1.call-done = f32[1024,768]{1,0:T(8,128)} async-done(((f32[1024,768]{1,0:T(8,128)}), f32[1024,768]{1,0:T(8,128)}) %all-reduce.11.cloned.1.call-update) | async-done | bytes 3145744 | tf_op jit(solution)/shard_map/psum | solution.py:73
  213.2 68.6 %all-reduce.13.cloned.1.call-done = f32[1024,768]{1,0:T(8,128)} async-done(((f32[1024,768]{1,0:T(8,128)}), f32[1024,768]{1,0:T(8,128)}) %all-reduce.13.cloned.1.call-update) | async-done | bytes 3145744 | tf_op jit(solution)/shard_map/psum | solution.py:77
  290.2 10.3 multiply_reduce_fusion.1
  302.4 6.6 multiply_convert_fusion.1
  334.0 6.9 fusion.59
  343.1 39.7 %all-reduce.15.cloned.1.call-done = f32[1024,768]{1,0:T(8,128)} async-done(((f32[1024,768]{1,0:T(8,128)}), f32[1024,768]{1,0:T(8,128)}) %all-reduce.15.cloned.1.call-update) | async-done | bytes 3145744 | tf_op jit(solution)/shard_map/psum | solution.py:203
  402.9 10.2 multiply_reduce_fusion
  415.7 6.6 multiply_convert_fusion
  438.6 10.7 reduce-scatter.19.cloned.1.call-done
  450.2 64.6 %reduce-scatter.21.cloned.1.call-done = f32[96,192]{1,0:T(8,128)} async-done(((f32[768,192]{1,0:T(8,128)}), f32[96,192]{1,0:T(8,128)}) %reduce-scatter.21.cloned.1.call-update) | async-done | bytes 73744 | tf_op jit(solution)/shard_map/reduce_scatter | solution.py:247
  521.3 61.4 %reduce-scatter.29.cloned.1.call-done = f32[96,512]{1,0:T(8,128)} async-done(((f32[768,512]{1,0:T(8,128)}), f32[96,512]{1,0:T(8,128)}) %reduce-scatter.29.cloned.1.call-update) | async-done | bytes 196624
  584.5 65.6 %reduce-scatter.27.cloned.1.call-done = f32[96,384]{1,0:T(8,128)} async-done(((f32[768,384]{1,0:T(8,128)}), f32[96,384]{1,0:T(8,128)}) %reduce-scatter.27.cloned.1.call-update) | async-done | bytes 147472
  652.2 63.7 %reduce-scatter.17.cloned.1.call-done = f32[96,192]{1,0:T(8,128)} async-done(((f32[768,192]{1,0:T(8,128)}), f32[96,192]{1,0:T(8,128)}) %reduce-scatter.17.cloned.1.call-update) | async-done | bytes 73744 | tf_op jit(solution)/shard_map/reduce_scatter | solution.py:244
  716.9 75.6 %reduce-scatter.23.cloned.1.call-done = f32[96,2,512]{2,0,1:T(8,128)} async-done(((f32[768,2,512]{2,0,1:T(8,128)}), f32[96,2,512]{2,0,1:T(8,128)}) %reduce-scatter.23.cloned.1.call-update) | async-done | bytes 393232 | tf_op jit(solution)/shard_map/reduce_scatter | solution.py:248
  795.8 69.2 %reduce-scatter.15.cloned.1.call-done = f32[96,3,192]{2,0,1:T(8,128)} async-done(((f32[768,3,192]{2,0,1:T(8,128)}), f32[96,3,192]{2,0,1:T(8,128)}) %reduce-scatter.15.cloned.1.call-update) | async-done | bytes 221200 | tf_op jit(solution)/shard_map/reduce_scatter | solution.py:243
  876.0 36.0 %all-reduce = (f32[]{:T(128)}, f32[576]{0:T(1024)}, f32[]{:T(128)}, f32[192]{0:T(256)}, f32[]{:T(128)}, /*index=5*/f32[192]{0:T(256)}, f32[]{:T(128)}, f32[384]{...) all-reduce(f32[]{:T(128)} %get-tuple-element.139, ...), channel_id=1, replica_groups=mesh['dp'=8,'mp'=4] {'dp'}, use_global_device_ids=true, to_apply=%region_38.39 | all-reduce | flops 3079 | bytes 24632 | tf_op jit(solution)/shard_map/psum | solution.py:97
  933.4 103.7 %all-reduce.17.cloned.1.call-done = (f32[1024,768]{1,0:T(8,128)}, f32[1024,768]{1,0:T(8,128)}, f32[1024,768]{1,0:T(8,128)}) async-done(((f32[1024,768]{1,0:T(8,128)}, f32[1024,768]{1,0:T(8,128)}, f32[1024,768]{1,0:T(8,128)}), (f32[1024,768]{1,0:T(8,128)}, f32[1024,768]{1,0:T(8,128)}, f32[1024,768]{1,0:T(8,128)})) %all-reduce.17.cloned.1.call-update) | async-done | bytes 9437200 | tf_op jit(solution)/shard_map/psum | solution.py:73
  1041.1 7.1 fusion.17
  1048.3 54.4 %reduce-scatter.25.cloned.1.call-done = f32[96,3]{1,0:T(8,128)} async-done(((f32[768,3]{1,0:T(8,128)}), f32[96,3]{1,0:T(8,128)}) %reduce-scatter.25.cloned.1.call-update) | async-done | bytes 1168
  (261 shorter events, 170.3 us)
Async XLA Ops:
  7.2 29.8 %copy-start = (bf16[1024,768]{1,0:T(8,128)(2,1)S(1)}, bf16[1024,768]{1,0:T(8,128)(2,1)}, u32[]{:S(2)}) copy-start(bf16[1024,768]{1,0:T(8,128)(2,1)} %param.14) | copy-start | bytes 4718596
  7.2 98.7 %all-reduce.9.cloned.1.call-start = ((), (), s32[]{:S(2)}) async-start(), calls=%async_computation.8 | async-start | bytes 6291456 | tf_op jit(solution)/shard_map/psum | solution.py:73
  34.7 71.3 %copy-start.9 = (bf16[1024,768]{1,0:T(8,128)(2,1)S(1)}, bf16[1024,768]{1,0:T(8,128)(2,1)}, u32[]{:S(2)}) copy-start(bf16[1024,768]{1,0:T(8,128)(2,1)} %param.13) | copy-start | bytes 4718596
  34.7 164.2 %all-reduce.11.cloned.1.call-start = ((), (), s32[]{:S(2)}) async-start(), calls=%async_computation.9 | async-start | bytes 6291456 | tf_op jit(solution)/shard_map/psum | solution.py:73
  130.2 151.7 %all-reduce.13.cloned.1.call-start = ((), (), s32[]{:S(2)}) async-start(), calls=%async_computation.10 | async-start | bytes 6291456 | tf_op jit(solution)/shard_map/psum | solution.py:77
  133.8 68.4 %copy-start.18 = (bf16[1024,768]{1,0:T(8,128)(2,1)S(1)}, bf16[1024,768]{1,0:T(8,128)(2,1)}, u32[]{:S(2)}) copy-start(bf16[1024,768]{1,0:T(8,128)(2,1)} %copy.69) | copy-start | bytes 4718596
  213.1 73.1 %copy-start.20 = (bf16[1024,768]{1,0:T(8,128)(2,1)S(1)}, bf16[1024,768]{1,0:T(8,128)(2,1)}, u32[]{:S(2)}) copy-start(bf16[1024,768]{1,0:T(8,128)(2,1)} %param.15) | copy-start | bytes 4718596
  213.1 169.7 %all-reduce.15.cloned.1.call-start = ((), (), s32[]{:S(2)}) async-start(), calls=%async_computation.11 | async-start | bytes 6291456 | tf_op jit(solution)/shard_map/psum | solution.py:203
  289.7 10.7 slice-start.3
  290.2 12.3 %slice-start.5 = ((s8[12582912]{0:T(1024)(128)(4,1)}), s8[4194304]{0:T(1024)(128)(4,1)S(1)}, s32[]{:S(2)}) async-start(s8[12582912]{0:T(1024)(128)(4,1)} %bitcast.183), calls=%async_computation.26 | async-start | bytes 8388608
  314.2 135.1 %reduce-scatter.19.cloned.1.call-start = ((), (), s32[]{:S(2)}) async-start(), calls=%async_computation.14 | async-start | bytes 884736 | tf_op jit(solution)/shard_map/reduce_scatter | solution.py:245
  317.9 196.9 %reduce-scatter.21.cloned.1.call-start = ((), (), s32[]{:S(2)}) async-start(), calls=%async_computation.15 | async-start | bytes 884736 | tf_op jit(solution)/shard_map/reduce_scatter | solution.py:247
  321.9 260.8 %reduce-scatter.29.cloned.1.call-start = ((), (), s32[]{:S(2)}) async-start(), calls=%async_computation.19 | async-start | bytes 1769472
  329.1 321.1 %reduce-scatter.27.cloned.1.call-start = ((), (), s32[]{:S(2)}) async-start(), calls=%async_computation.18 | async-start | bytes 1327104
  343.1 372.8 %reduce-scatter.17.cloned.1.call-start = ((), (), s32[]{:S(2)}) async-start(), calls=%async_computation.13 | async-start | bytes 884736 | tf_op jit(solution)/shard_map/reduce_scatter | solution.py:244
  393.4 399.1 %reduce-scatter.23.cloned.1.call-start = ((), (), s32[]{:S(2)}) async-start(), calls=%async_computation.16 | async-start | bytes 3538944 | tf_op jit(solution)/shard_map/reduce_scatter | solution.py:248
  399.4 465.5 %reduce-scatter.15.cloned.1.call-start = ((), (), s32[]{:S(2)}) async-start(), calls=%async_computation.12 | async-start | bytes 2654208 | tf_op jit(solution)/shard_map/reduce_scatter | solution.py:243
  402.9 11.5 %slice-start.1 = ((s8[12582912]{0:T(1024)(128)(4,1)}), s8[4194304]{0:T(1024)(128)(4,1)S(1)}, s32[]{:S(2)}) async-start(s8[12582912]{0:T(1024)(128)(4,1)} %bitcast.181), calls=%async_computation.22 | async-start | bytes 8388608
  402.9 12.7 %slice-start.2 = ((s8[12582912]{0:T(1024)(128)(4,1)}), s8[4194304]{0:T(1024)(128)(4,1)S(1)}, s32[]{:S(2)}) async-start(s8[12582912]{0:T(1024)(128)(4,1)} %bitcast.181), calls=%async_computation.23 | async-start | bytes 8388608
  431.5 605.6 %all-reduce.17.cloned.1.call-start = ((), (), s32[]{:S(2)}) async-start(), calls=%async_computation.20 | async-start | bytes 18874368 | tf_op jit(solution)/shard_map/psum | solution.py:73
  435.8 80.0 %copy-start.52 = (f32[768]{0:T(1024)S(1)}, f32[768]{0:T(1024)}, u32[]{:S(2)}) copy-start(f32[768]{0:T(1024)} %get-tuple-element.72) | copy-start | bytes 9220
  521.1 581.6 %reduce-scatter.25.cloned.1.call-start = ((), (), s32[]{:S(2)}) async-start(), calls=%async_computation.17 | async-start | bytes 442368
  921.2 118.9 %copy-start.53 = (f32[768,1]{0,1:T(1,128)S(1)}, f32[768,1]{0,1:T(1,128)}, u32[]{:S(2)}) copy-start(f32[768,1]{0,1:T(1,128)} %stack.56) | copy-start | bytes 9220
  930.0 111.1 %copy-start.43 = (f32[1024]{0:T(1024)S(1)}, f32[1024]{0:T(1024)}, u32[]{:S(2)}) copy-start(f32[1024]{0:T(1024)} %copy-done.42) | copy-start | bytes 12292
  (57 other events, 209.9 us)
Sparse Core Ops, SparseCore 0:
  34.8 71.1 all-reduce.8
  130.3 68.5 all-reduce.10
  213.3 68.5 all-reduce.12
  314.3 68.5 all-reduce.14
  386.6 62.6 reduce-scatter.18
  453.3 61.4 reduce-scatter.20
  518.8 63.8 reduce-scatter.28
  587.1 62.9 reduce-scatter.26
  654.3 61.4 reduce-scatter.16
  719.3 73.1 reduce-scatter.22
  796.6 68.2 reduce-scatter.14
  867.5 169.5 all-reduce.16
  1041.2 61.3 reduce-scatter.24
where the time goes:
time: 1120 us; the launch traced here: 1110 us
  waiting for transfers between devices  809 us (72%)
  matrix products  132 us (12%)
  other arithmetic  69.3 us (6%)
  local copies, waits for them, and re-layouts  41.8 us (4%)
  blocking collectives  41.6 us (4%)
  between operations  19.4 us (2%)
    psum x3, waiting for transfers between devices, branch_total(): return lax.psum(partial_out, 'mp')  235 us
    unnamed x16, waiting for transfers between devices  182 us
    reduce_scatter x1, waiting for transfers between devices, on_device(): lax.psum_scatter(partials[6], 'dp', scatter_dimension=0, tiled=True)  75.6 us
    reduce_scatter x1, waiting for transfers between devices, on_device(): lax.psum_scatter(partials[1], 'dp', scatter_dimension=0, tiled=True)  69.2 us
    psum x1, waiting for transfers between devices, input_total(): return lax.psum(partial_grad, 'mp')  68.6 us
    reduce_scatter x1, waiting for transfers between devices, on_device(): lax.psum_scatter(partials[5], 'dp', scatter_dimension=0, tiled=True)  64.6 us
    reduce_scatter x1, waiting for transfers between devices, on_device(): lax.psum_scatter(partials[2], 'dp', scatter_dimension=0, tiled=True)  63.7 us
    psum x1, waiting for transfers between devices, on_device(): grad_normed_b, grad_memory = lax.psum((part_normed, part_memory), 'mp')  39.7 us
  transfers between devices with their start and end apart: 13, of which 13 were waited for; matrix products, arithmetic and copies ran while one was open for 12% of the time, Pallas kernels for 0%

commit v1 on v0

v1 whole, which is shorter than its diff:
```python
import functools
import math

import jax
import jax.numpy as jnp
from jax import lax
from jax.experimental import pallas as pl
from jax.experimental.pallas import tpu as pltpu
from jax.sharding import PartitionSpec as P

DH = 64
PATCH = 256
LONGEST = 512
ROWS = 256
SPAN = LONGEST // ROWS
F32 = jnp.float32
BF16 = jnp.bfloat16
NEG = -1e30
SCALE = 1.0 / math.sqrt(DH)
VMEM_BYTES = 56 * 1024 * 1024


def nn(a, b):
    return lax.dot_general(a, b, (((1,), (0,)), ((), ())), preferred_element_type=F32)


def nt(a, b):
    return lax.dot_general(a, b, (((1,), (1,)), ((), ())), preferred_element_type=F32)


def tn(a, b):
    return lax.dot_general(a, b, (((0,), (0,)), ((), ())), preferred_element_type=F32)


def normed_of(rows, gain):
    return rows * lax.rsqrt(jnp.mean(rows * rows, axis=-1, keepdims=True) + 1e-06) * gain


def norm_vjp(rows, gain, grad):
    inv = lax.rsqrt(jnp.mean(rows * rows, axis=-1, keepdims=True) + 1e-06)
    scaled = rows * inv
    hg = grad * gain
    inner = jnp.mean(hg * scaled, axis=-1, keepdims=True)
    grad_rows = inv * (hg - scaled * inner)
    grad_gain = jnp.sum(grad * scaled, axis=0, keepdims=True)
    return grad_rows, grad_gain, scaled


def place_pieces(dst, base, ctl, by_y, by_x, by_z):
    q = by_x.shape[0]
    x, z = ctl[0], ctl[1]

    def at(offset):
        return pl.ds(pl.multiple_of(offset, 64), q)

    dst[at(base + x * q), :] = by_y[:q, :].astype(BF16)
    dst[at(base + (1 - x) * q), :] = by_x[...].astype(BF16)
    dst[at(base + (2 + z) * q), :] = by_y[q:, :].astype(BF16)
    dst[at(base + (3 - z) * q), :] = by_z[...].astype(BF16)


def table_ends(lengths):
    ends = []
    total = lengths[0, 0]
    for j in range(1, lengths.shape[1]):
        ends.append(total)
        total = total + lengths[0, j]
    return ends


def query_places(base):
    return lax.broadcasted_iota(jnp.int32, (1, ROWS), 1) + base


def self_bias(lengths, base, low, width):
    places = query_places(base)
    start = jnp.zeros_like(places)
    for end in table_ends(lengths):
        start = jnp.where(places >= end, end, start)
    keys = lax.broadcasted_iota(jnp.int32, (width, ROWS), 0) + low
    return jnp.where((keys >= start) & (keys <= places), 0.0, NEG)


def window_cases(block, body):
    for back in range(SPAN + 1):
        width = (back + 1) * ROWS

        @pl.when(block == back if back < SPAN else block >= SPAN)
        def _run(back=back, width=width):
            if back < SPAN:
                body(0, width)
            else:
                body(pl.multiple_of((block - SPAN) * ROWS, ROWS), width)


def full(shape):
    return pl.BlockSpec(shape, lambda i: (0,) * len(shape))


def by_rows(width):
    return pl.BlockSpec((ROWS, width), lambda i: (i, 0))


def by_cols(height):
    return pl.BlockSpec((height, ROWS), lambda i: (0, i))


SMEM = pl.BlockSpec(memory_space=pltpu.SMEM)


def run(kernel, grid, ins, outs, scratch, flops, name, transcendentals=0):
    arrays = [a for a, _ in ins]
    moved = sum(a.size * a.dtype.itemsize for a in arrays) + sum(
        math.prod(s.shape) * jnp.dtype(s.dtype).itemsize for s, _ in outs
    )
    return pl.pallas_call(
        kernel,
        grid=(grid,),
        in_specs=[s for _, s in ins],
        out_specs=[s for _, s in outs],
        out_shape=[s for s, _ in outs],
        scratch_shapes=scratch,
        compiler_params=pltpu.CompilerParams(
            vmem_limit_bytes=VMEM_BYTES, dimension_semantics=("arbitrary",)
        ),
        cost_estimate=pl.CostEstimate(
            flops=flops, bytes_accessed=moved, transcendentals=transcendentals
        ),
        name=name,
    )(*arrays)


def sds(shape, dtype):
    return jax.ShapeDtypeStruct(shape, dtype)


def self_forward_kernel(remote, heads, *refs):
    if remote:
        (lengths, ctl, tokens, gain, by_y, by_x, by_z, base_out) = refs[:8]
        (qkv_t, mixed_t, lse, out, w_out, k_rows) = refs[8:]
        w = w_out
    else:
        (lengths, tokens, gain, w) = refs[:4]
        (qkv_t, mixed_t, lse, out, k_rows) = refs[4:]
    block = pl.program_id(0)
    hq = heads * DH
    if remote:

        @pl.when(block == 0)
        def _place():
            place_pieces(w, 0, ctl, by_y, by_x, by_z)

    base = pl.multiple_of(block * ROWS, ROWS)
    here = pl.ds(base, ROWS)
    normed = normed_of(tokens[...].astype(F32), gain[...]).astype(BF16)
    qkv = nt(w[0 : 3 * hq, :], normed).astype(BF16)
    q_all = (qkv[:hq].astype(F32) * SCALE).astype(BF16)
    qkv_t[0:hq, here] = q_all
    qkv_t[hq : 3 * hq, here] = qkv[hq:]
    for h in range(heads):
        k_rows[h, here, :] = qkv[hq + h * DH : hq + (h + 1) * DH].T

    def attend(low, width):
        window = pl.ds(low, width)
        bias = self_bias(lengths, base, low, width)
        for h in range(heads):
            own = slice(h * DH, (h + 1) * DH)
            s = nn(k_rows[h, window, :], q_all[own]) + bias
            top = jnp.max(s, axis=0, keepdims=True)
            e = jnp.exp(s - top)
            total = jnp.sum(e, axis=0, keepdims=True)
            o = nn(qkv_t[2 * hq + h * DH : 2 * hq + (h + 1) * DH, window], e.astype(BF16))
            mixed_t[own, :] = (o * (1.0 / total)).astype(BF16)
            lse[h : h + 1, :] = top + jnp.log(total)

    window_cases(block, attend)
    part = tn(mixed_t[...], w[3 * hq : 4 * hq, :])
    out[...] = part + base_out[...] if remote else part


def self_forward(lengths, tokens, gain, w, heads, remote=None):
    slots, width = tokens.shape
    hq = heads * DH
    outs = [
        (sds((3 * hq, slots), BF16), full((3 * hq, slots))),
        (sds((hq, slots), BF16), by_cols(hq)),
        (sds((8, slots), F32), by_cols(8)),
        (sds((slots, width), F32), by_rows(width)),
    ]
    scratch = [pltpu.VMEM((heads, slots, DH), BF16)]
    if remote is None:
        ins = [(lengths, SMEM), (tokens, by_rows(width)), (gain, full(gain.shape)), (w, full(w.shape))]
    else:
        ctl, by_y, by_x, by_z, base_out = remote
        ins = [
            (lengths, SMEM),
            (ctl, SMEM),
            (tokens, by_rows(width)),
            (gain, full(gain.shape)),
            (by_y, full(by_y.shape)),
            (by_x, full(by_x.shape)),
            (by_z, full(by_z.shape)),
            (base_out, by_rows(width)),
        ]
        outs.append((sds((4 * hq, width), BF16), full((4 * hq, width))))
    flops = 2 * slots * width * 4 * hq + heads * 4 * slots * slots * DH
    return run(
        functools.partial(self_forward_kernel, remote is not None, heads),
        slots // ROWS, ins, outs, scratch, flops, "self_forward", heads * slots * slots,
    )


def memory_kernel(remote, heads, *refs):
    hq = heads * DH
    if remote:
        ctl, memory, by_y, by_x, by_z, kv_t, k_rows, v_rows, w = refs

        @pl.when(pl.program_id(0) == 0)
        def _place():
            place_pieces(w, 0, ctl, by_y, by_x, by_z)
    else:
        memory, w, kv_t, k_rows, v_rows = refs
    kv = nt(w[hq : 3 * hq, :], memory[...]).astype(BF16)
    kv_t[...] = kv
    for h in range(heads):
        k_rows[h] = kv[h * DH : (h + 1) * DH].T
        v_rows[h] = kv[hq + h * DH : hq + (h + 1) * DH].T


def memory_forward(memory, w, heads, remote=None):
    count, width = memory.shape
    hq = heads * DH
    head_rows = pl.BlockSpec((heads, ROWS, DH), lambda i: (0, i, 0))
    outs = [
        (sds((2 * hq, count), BF16), by_cols(2 * hq)),
        (sds((heads, count, DH), BF16), head_rows),
        (sds((heads, count, DH), BF16), head_rows),
    ]
    if remote is None:
        ins = [(memory, by_rows(width)), (w, full(w.shape))]
    else:
        ctl, by_y, by_x, by_z = remote
        ins = [
            (ctl, SMEM),
            (memory, by_rows(width)),
            (by_y, full(by_y.shape)),
            (by_x, full(by_x.shape)),
            (by_z, full(by_z.shape)),
        ]
        outs.append((sds((4 * hq, width), BF16), full((4 * hq, width))))
    return run(
        functools.partial(memory_kernel, remote is not None, heads),
        count // ROWS, ins, outs, [], 2 * count * width * 2 * hq, "memory_forward",
    )


def tables_of_block(lengths, base, body):
    ends = table_ends(lengths)
    places = query_places(base)
    segment = jnp.zeros_like(places)
    first_table = jnp.int32(0)
    last_table = jnp.int32(0)
    for end in ends:
        segment = segment + (places >= end).astype(jnp.int32)
        first_table = first_table + (base >= end).astype(jnp.int32)
        last_table = last_table + (base + ROWS - 1 >= end).astype(jnp.int32)

    def step(table, carry):
        body(table, segment == table)
        return carry

    lax.fori_loop(first_table, last_table + 1, step, 0)


def cross_forward_kernel(leading, heads, *refs):
    hq = heads * DH
    if leading:
        (lengths, plots, tokens, part, other, gain, w, kv_t, k_rows) = refs[:9]
        (q_t, mixed_t, lse, out, first, normed_out) = refs[9:]
        rows = tokens[...].astype(F32) + (part[...] + other[...])
        first[...] = rows
        normed = normed_of(rows, gain[...]).astype(BF16)
        normed_out[...] = normed
    else:
        (lengths, plots, normed_in, w, kv_t, k_rows, base_out) = refs[:7]
        (q_t, mixed_t, lse, out) = refs[7:]
        normed = normed_in[...]
    base = pl.multiple_of(pl.program_id(0) * ROWS, ROWS)
    query = nt(w[0:hq, :], normed).astype(BF16)
    q_all = (query.astype(F32) * SCALE).astype(BF16)
    q_t[...] = q_all

    def table(j, member):
        plot = pl.ds(pl.multiple_of(plots[0, j] * PATCH, PATCH), PATCH)
        for h in range(heads):
            own = slice(h * DH, (h + 1) * DH)
            s = nn(k_rows[h, plot, :], q_t[own, :])
            top = jnp.max(s, axis=0, keepdims=True)
            e = jnp.exp(s - top)
            total = jnp.sum(e, axis=0, keepdims=True)
            o = nn(kv_t[hq + h * DH : hq + (h + 1) * DH, plot], e.astype(BF16))
            o = o * (1.0 / total)
            mixed_t[own, :] = jnp.where(member, o, mixed_t[own, :].astype(F32)).astype(BF16)
            lse[h : h + 1, :] = jnp.where(member, top + jnp.log(total), lse[h : h + 1, :])

    tables_of_block(lengths, base, table)
    part_out = tn(mixed_t[...], w[3 * hq : 4 * hq, :])
    out[...] = part_out if leading else part_out + base_out[...]


def cross_forward(lengths, plots, w, kv_t, k_rows, heads, lead=None, follow=None):
    hq = heads * DH
    slots = (lead or follow)[0].shape[0]
    width = w.shape[1]
    outs = [
        (sds((hq, slots), BF16), by_cols(hq)),
        (sds((hq, slots), BF16), by_cols(hq)),
        (sds((8, slots), F32), by_cols(8)),
        (sds((slots, width), F32), by_rows(width)),
    ]
    shared = [(w, full(w.shape)), (kv_t, full(kv_t.shape)), (k_rows, full(k_rows.shape))]
    if lead is not None:
        tokens, part, other, gain = lead
        ins = [
            (lengths, SMEM),
            (plots, SMEM),
            (tokens, by_rows(width)),
            (part, by_rows(width)),
            (other, by_rows(width)),
            (gain, full(gain.shape)),
        ] + shared
        outs += [
            (sds((slots, width), F32), by_rows(width)),
            (sds((slots, width), BF16), by_rows(width)),
        ]
    else:
        normed, base_out = follow
        ins = [(lengths, SMEM), (plots, SMEM), (normed, by_rows(width))] + shared
        ins.append((base_out, by_rows(width)))
    flops = 2 * slots * width * 2 * hq + heads * 8 * slots * PATCH * DH
    return run(
        functools.partial(cross_forward_kernel, lead is not None, heads),
        slots // ROWS, ins, outs, [], flops, "cross_forward", heads * slots * PATCH * 2,
    )


def feed_kernel(leading, units, *refs):
    if leading:
        (first, part, other, gain, cot, w) = refs[:6]
        (result, grad_in, second, normed_out, dw) = refs[6:]
        rows = first[...] + (part[...] + other[...])
        second[...] = rows
        normed = normed_of(rows, gain[...]).astype(BF16)
        normed_out[...] = normed

        @pl.when(pl.program_id(0) == 0)
        def _zero():
            dw[...] = jnp.zeros_like(dw)
    else:
        (ctl, normed_in, cot, y0, x0, z0, y1, x1, z1, base_result, base_grad) = refs[:11]
        (result, grad_in, w) = refs[11:]
        normed = normed_in[...]

        @pl.when(pl.program_id(0) == 0)
        def _place():
            place_pieces(w, 0, ctl, y0, x0, z0)
            place_pieces(w, 4 * x0.shape[0], ctl, y1, x1, z1)

    cot_rows = cot[...]
    gate_up = nt(normed, w[0 : 2 * units, :])
    gate, up = gate_up[:, :units], gate_up[:, units:]
    c0 = math.sqrt(2.0 / math.pi)
    square = gate * gate
    th = jnp.tanh(c0 * gate * (1.0 + 0.044715 * square))
    half = 0.5 * (1.0 + th)
    gelu = gate * half
    slope = half + (0.5 * c0) * gate * (1.0 - th * th) * (1.0 + (3 * 0.044715) * square)
    hidden = (gelu * up).astype(BF16)
    res = nn(hidden, w[2 * units : 3 * units, :])
    grad_hidden = nt(cot_rows, w[2 * units : 3 * units, :])
    grad_gate = (grad_hidden * up * slope).astype(BF16)
    grad_up = (grad_hidden * gelu).astype(BF16)
    back = nn(grad_gate, w[0:units, :]) + nn(grad_up, w[units : 2 * units, :])
    if leading:
        result[...] = res
        grad_in[...] = back
        dw[:, 0:units] += tn(normed, grad_gate)
        dw[:, units : 2 * units] += tn(normed, grad_up)
        dw[:, 2 * units : 3 * units] += tn(cot_rows, hidden)
    else:
        result[...] = res + base_result[...]
        grad_in[...] = back + base_grad[...]


def feed(units, lead=None, follow=None):
    if lead is not None:
        first, part, other, gain, cot, w = lead
        slots, width = first.shape
        ins = [
            (first, by_rows(width)),
            (part, by_rows(width)),
            (other, by_rows(width)),
            (gain, full(gain.shape)),
            (cot, by_rows(width)),
            (w, full(w.shape)),
        ]
    else:
        ctl, normed, cot, pieces, base_result, base_grad = follow
        slots, width = normed.shape
        ins = [(ctl, SMEM), (normed, by_rows(width)), (cot, by_rows(width))]
        ins += [(piece, full(piece.shape)) for piece in pieces]
        ins += [(base_result, by_rows(width)), (base_grad, by_rows(width))]
    outs = [
        (sds((slots, width), F32), by_rows(width)),
        (sds((slots, width), F32), by_rows(width)),
    ]
    scratch = []
    if lead is not None:
        outs += [
            (sds((slots, width), F32), by_rows(width)),
            (sds((slots, width), BF16), by_rows(width)),
            (sds((width, 3 * units), F32), full((width, 3 * units))),
        ]
    else:
        scratch = [pltpu.VMEM((3 * units, width), BF16)]
    flops = 2 * slots * width * units * (9 if lead is not None else 6)
    return run(
        functools.partial(feed_kernel, lead is not None, units),
        slots // ROWS, ins, outs, scratch, flops, "feed", slots * units,
    )


def cross_backward_kernel(leading, heads, *refs):
    hq = heads * DH
    if leading:
        (lengths, plots, second, part, other, cot, gain, normed, memory) = refs[:9]
        (w, q_t, mixed_t, lse, kv_t, k_rows, v_rows) = refs[9:16]
        (grad_in, grad_mem, grad_second, branch_out, grad_gain, dw) = refs[16:22]
        (dkv, dq, dm, dw_t) = refs[22:]
    else:
        (lengths, plots, branch_in, w, q_t, lse, kv_t, k_rows, v_rows, base_grad, base_mem) = refs[:11]
        (grad_in, grad_mem, dkv, dq, dm) = refs[11:]
    block = pl.program_id(0)
    last = pl.num_programs(0) - 1
    base = pl.multiple_of(block * ROWS, ROWS)

    @pl.when(block == 0)
    def _zero():
        dkv[...] = jnp.zeros_like(dkv)
        if leading:
            dw_t[...] = jnp.zeros_like(dw_t)
            grad_gain[...] = jnp.zeros_like(grad_gain)

    if leading:
        grad_rows, gain_rows, _ = norm_vjp(second[...], gain[...], part[...] + other[...])
        total = cot[...].astype(F32) + grad_rows
        grad_second[...] = total
        branch = total.astype(BF16)
        branch_out[...] = branch
        grad_gain[0:1, :] += gain_rows
    else:
        branch = branch_in[...]
    dm[...] = nt(w[3 * hq : 4 * hq, :], branch).astype(BF16)
    dq[...] = jnp.zeros_like(dq)

    def table(j, member):
        plot = pl.ds(pl.multiple_of(plots[0, j] * PATCH, PATCH), PATCH)
        for h in range(heads):
            own = slice(h * DH, (h + 1) * DH)
            val = slice(hq + h * DH, hq + (h + 1) * DH)
            query = q_t[own, :]
            dmix = jnp.where(member, dm[own, :].astype(F32), 0.0).astype(BF16)
            level = jnp.where(member, lse[h : h + 1, :], -NEG)
            p = jnp.exp(nn(k_rows[h, plot, :], query) - level)
            dp = nn(v_rows[h, plot, :], dmix)
            inner = jnp.sum(p * dp, axis=0, keepdims=True)
            ds = (p * (dp - inner)).astype(BF16)
            dkv[own, plot] += nt(query, ds)
            dkv[val, plot] += nt(dmix, p.astype(BF16))
            dq[own, :] += nn(kv_t[own, plot], ds)

    tables_of_block(lengths, base, table)
    grad_query = (dq[...] * SCALE).astype(BF16)
    back = tn(grad_query, w[0:hq, :])
    grad_in[...] = back if leading else back + base_grad[...]
    if leading:
        dw_t[0:hq, :] += nn(grad_query, normed[...])
        dw_t[3 * hq : 4 * hq, :] += nn(mixed_t[...], branch)

    @pl.when(block == last)
    def _finish():
        for m in range(dkv.shape[1] // ROWS):
            here = slice(m * ROWS, (m + 1) * ROWS)
            rows = dkv[:, here].astype(BF16)
            back_mem = tn(rows, w[hq : 3 * hq, :])
            grad_mem[here, :] = back_mem if leading else back_mem + base_mem[here, :]
            if leading:
                dw_t[hq : 3 * hq, :] += nn(rows, memory[here, :])
        if leading:
            dw[...] = dw_t[...].T


def cross_backward(lengths, plots, w, q_t, lse, kv_t, k_rows, v_rows, heads, lead=None, follow=None):
    hq = heads * DH
    slots, width = q_t.shape[1], w.shape[1]
    count = kv_t.shape[1]
    outs = [
        (sds((slots, width), F32), by_rows(width)),
        (sds((count, width), F32), full((count, width))),
    ]
    scratch = [
        pltpu.VMEM((2 * hq, count), F32),
        pltpu.VMEM((hq, ROWS), F32),
        pltpu.VMEM((hq, ROWS), BF16),
    ]
    heads_part = [
        (lse, by_cols(8)),
        (kv_t, full(kv_t.shape)),
        (k_rows, full(k_rows.shape)),
        (v_rows, full(v_rows.shape)),
    ]
    if lead is not None:
        second, part, other, cot, gain, normed, memory, mixed_t = lead
        ins = [
            (lengths, SMEM),
            (plots, SMEM),
            (second, by_rows(width)),
            (part, by_rows(width)),
            (other, by_rows(width)),
            (cot, by_rows(width)),
            (gain, full(gain.shape)),
            (normed, by_rows(width)),
            (memory, full(memory.shape)),
            (w, full(w.shape)),
            (q_t, by_cols(hq)),
            (mixed_t, by_cols(hq)),
        ] + heads_part
        outs += [
            (sds((slots, width), F32), by_rows(width)),
            (sds((slots, width), BF16), by_rows(width)),
            (sds((8, width), F32), full((8, width))),
            (sds((width, 4 * hq), F32), full((width, 4 * hq))),
        ]
        scratch.append(pltpu.VMEM((4 * hq, width), F32))
    else:
        branch, base_grad, base_mem = follow
        ins = [
            (lengths, SMEM),
            (plots, SMEM),
            (branch, by_rows(width)),
            (w, full(w.shape)),
            (q_t, by_cols(hq)),
        ] + heads_part
        ins += [(base_grad, by_rows(width)), (base_mem, full(base_mem.shape))]
    flops = 2 * slots * width * hq * (8 if lead is not None else 4) + heads * 20 * slots * PATCH * DH
    return run(
        functools.partial(cross_backward_kernel, lead is not None, heads),
        slots // ROWS, ins, outs, scratch, flops, "cross_backward", heads * slots * PATCH * 2,
    )


def self_backward_kernel(leading, heads, *refs):
    hq = heads * DH
    if leading:
        (lengths, first, part, other, carried, gain, tokens, gain_in, w, qkv_t, mixed_t, lse) = refs[:12]
        (grad_in, grad_first, branch_out, grad_gain, dw) = refs[12:17]
        (dkv, k_rows, v_rows, dqkv, dw_t) = refs[17:]
    else:
        (lengths, branch_in, w, qkv_t, lse, base_grad) = refs[:6]
        (grad_in, dkv, k_rows, v_rows, dqkv) = refs[6:]
    step = pl.program_id(0)
    last = pl.num_programs(0) - 1
    block = last - step
    base = pl.multiple_of(block * ROWS, ROWS)
    here = pl.ds(base, ROWS)

    @pl.when(step == 0)
    def _start():
        dkv[...] = jnp.zeros_like(dkv)
        for h in range(heads):
            k_rows[h] = qkv_t[hq + h * DH : hq + (h + 1) * DH, :].T
            v_rows[h] = qkv_t[2 * hq + h * DH : 2 * hq + (h + 1) * DH, :].T
        if leading:
            dw_t[...] = jnp.zeros_like(dw_t)
            grad_gain[...] = jnp.zeros_like(grad_gain)

    if leading:
        grad_rows, gain_rows, _ = norm_vjp(first[...], gain[...], part[...] + other[...])
        total = carried[...] + grad_rows
        grad_first[...] = total
        branch = total.astype(BF16)
        branch_out[...] = branch
        grad_gain[0:1, :] += gain_rows
    else:
        branch = branch_in[...]
    dm_all = nt(w[3 * hq : 4 * hq, :], branch).astype(BF16)

    def attend(low, width):
        window = pl.ds(low, width)
        bias = self_bias(lengths, base, low, width)
        for h in range(heads):
            own = slice(h * DH, (h + 1) * DH)
            key = slice(hq + h * DH, hq + (h + 1) * DH)
            val = slice(hq + h * DH, hq + (h + 1) * DH)
            query = qkv_t[own, here]
            dmix = dm_all[own]
            p = jnp.exp(nn(k_rows[h, window, :], query) + bias - lse[h : h + 1, :])
            dp = nn(v_rows[h, window, :], dmix)
            inner = jnp.sum(p * dp, axis=0, keepdims=True)
            ds = (p * (dp - inner)).astype(BF16)
            dkv[own, window] += nt(query, ds)
            dkv[val, window] += nt(dmix, p.astype(BF16))
            dqkv[own, :] = (nn(qkv_t[key, window], ds) * SCALE).astype(BF16)

    window_cases(block, attend)
    dqkv[hq : 3 * hq, :] = dkv[:, here].astype(BF16)
    rows = dqkv[...]
    back = tn(rows, w[0 : 3 * hq, :])
    grad_in[...] = back if leading else back + base_grad[...]
    if leading:
        normed = normed_of(tokens[...].astype(F32), gain_in[...]).astype(BF16)
        dw_t[0 : 3 * hq, :] += nn(rows, normed)
        dw_t[3 * hq : 4 * hq, :] += nn(mixed_t[...], branch)

        @pl.when(step == last)
        def _finish():
            dw[...] = dw_t[...].T


def self_backward(lengths, w, qkv_t, lse, heads, lead=None, follow=None):
    hq = heads * DH
    slots, width = qkv_t.shape[1], w.shape[1]
    last = slots // ROWS - 1
    rows = pl.BlockSpec((ROWS, width), lambda i: (last - i, 0))

    def cols(height):
        return pl.BlockSpec((height, ROWS), lambda i: (0, last - i))

    outs = [(sds((slots, width), F32), rows)]
    scratch = [
        pltpu.VMEM((2 * hq, slots), F32),
        pltpu.VMEM((heads, slots, DH), BF16),
        pltpu.VMEM((heads, slots, DH), BF16),
        pltpu.VMEM((3 * hq, ROWS), BF16),
    ]
    if lead is not None:
        first, part, other, carried, gain, tokens, gain_in, mixed_t = lead
        ins = [
            (lengths, SMEM),
            (first, rows),
            (part, rows),
            (other, rows),
            (carried, rows),
            (gain, full(gain.shape)),
            (tokens, rows),
            (gain_in, full(gain_in.shape)),
            (w, full(w.shape)),
            (qkv_t, full(qkv_t.shape)),
            (mixed_t, cols(hq)),
            (lse, cols(8)),
        ]
        outs += [
            (sds((slots, width), F32), rows),
            (sds((slots, width), BF16), rows),
            (sds((8, width), F32), full((8, width))),
            (sds((width, 4 * hq), F32), full((width, 4 * hq))),
        ]
        scratch.append(pltpu.VMEM((4 * hq, width), F32))
    else:
        branch, base_grad = follow
        ins = [
            (lengths, SMEM),
            (branch, rows),
            (w, full(w.shape)),
            (qkv_t, full(qkv_t.shape)),
            (lse, cols(8)),
            (base_grad, rows),
        ]
    flops = 2 * slots * width * hq * (8 if lead is not None else 4) + heads * 10 * slots * slots * DH
    return run(
        functools.partial(self_backward_kernel, lead is not None, heads),
        slots // ROWS, ins, outs, scratch, flops, "self_backward", heads * slots * slots,
    )


def tail_kernel(tokens, part, other, carried, gain, grad_tokens, grad_gain):
    @pl.when(pl.program_id(0) == 0)
    def _zero():
        grad_gain[...] = jnp.zeros_like(grad_gain)

    grad_rows, gain_rows, _ = norm_vjp(tokens[...].astype(F32), gain[...], part[...] + other[...])
    grad_tokens[...] = carried[...] + grad_rows
    grad_gain[0:1, :] += gain_rows


def tail(tokens, part, other, carried, gain):
    slots, width = tokens.shape
    ins = [
        (tokens, by_rows(width)),
        (part, by_rows(width)),
        (other, by_rows(width)),
        (carried, by_rows(width)),
        (gain, full(gain.shape)),
    ]
    outs = [
        (sds((slots, width), F32), by_rows(width)),
        (sds((8, width), F32), full((8, width))),
    ]
    return run(tail_kernel, slots // ROWS, ins, outs, [], 20 * slots * width, "last_norm")


def swap(value, axis, bit):
    count = lax.axis_size(axis)
    return lax.ppermute(value, axis, [(i, i ^ bit) for i in range(count)])


def fetch_quarter(w, x, z):
    quarter = w.shape[0] // 4
    pieces = w.reshape(4, quarter, w.shape[1])
    mine = jnp.concatenate(
        [jnp.where(x == 0, pieces[0], pieces[1]), jnp.where(z == 0, pieces[2], pieces[3])], axis=0
    )
    by_y = swap(mine.astype(F32), "mp", 2)
    by_x = swap(by_y[:quarter], "dp", 1)
    by_z = swap(by_y[quarter:], "dp", 2)
    return by_y, by_x, by_z


def scatter_rows(grad):
    place = lax.axis_index("dp")
    count = lax.axis_size("dp")
    own_rows = grad.shape[0] // count
    width = grad.shape[1]
    bit = 1
    left = count
    while bit < count:
        mine = (place // bit) % 2
        halves = grad.reshape(left // 2, 2, own_rows, width)
        sent = lax.dynamic_index_in_dim(halves, 1 - mine, axis=1, keepdims=False)
        kept = lax.dynamic_index_in_dim(halves, mine, axis=1, keepdims=False)
        grad = (kept + swap(sent, "dp", bit)).reshape(left // 2 * own_rows, width)
        left //= 2
        bit *= 2
    return grad


def all_sum(value, axis):
    bit = 1
    while bit < lax.axis_size(axis):
        value = value + swap(value, axis, bit)
        bit *= 2
    return value


def adafactor(pieces, model_width, extra=None):
    ways = lax.axis_size("mp")
    row_sums = all_sum(jnp.stack([jnp.sum(g * g, axis=1) for g in pieces], axis=0), "mp")
    row_means = [
        row_sums[k] / (g.shape[1] * ways) + 1e-30 for k, g in enumerate(pieces)
    ]
    parts = [jnp.sum(g * g, axis=0) for g in pieces]
    parts.append(jnp.stack([jnp.sum(m) for m in row_means]))
    if extra is not None:
        parts.append(extra)
    summed = all_sum(jnp.concatenate(parts), "dp")
    steps = []
    at = 0
    tail_at = sum(g.shape[1] for g in pieces)
    for k, g in enumerate(pieces):
        col_mean = summed[at : at + g.shape[1]] / model_width + 1e-30
        at += g.shape[1]
        mean_rows = summed[tail_at + k] / model_width
        factor = row_means[k][:, None] * col_mean[None, :] / mean_rows
        steps.append(g * lax.rsqrt(factor))
    if extra is None:
        return steps
    return steps, summed[tail_at + len(pieces) :]


def on_device(
    tokens,
    memory,
    cotangent,
    table_lengths,
    table_plots,
    gains,
    w_qkv,
    w_self_out,
    w_cross_query,
    w_cross_kv,
    w_cross_out,
    w_gate_up,
    w_down,
):
    slots, width = tokens.shape
    hq = w_self_out.shape[1]
    heads = hq // DH
    units = w_down.shape[1]
    place = lax.axis_index("dp")
    x, z = place % 2, (place // 2) % 2
    ctl = jnp.stack([x, z]).astype(jnp.int32)
    gain_rows = gains.T
    gain_a, gain_b, gain_c = gain_rows[0:1], gain_rows[1:2], gain_rows[2:3]

    w_a = jnp.concatenate([w_qkv.transpose(1, 2, 0).reshape(3 * hq, width), w_self_out.T], axis=0)
    w_b = jnp.concatenate(
        [w_cross_query.T, w_cross_kv.transpose(1, 2, 0).reshape(2 * hq, width), w_cross_out.T], axis=0
    )
    w_f = jnp.concatenate(
        [w_gate_up.transpose(1, 2, 0).reshape(2 * units, width), w_down.T], axis=0
    )
    half_f = w_f.shape[0] // 2
    far_a = fetch_quarter(w_a, x, z)
    far_b = fetch_quarter(w_b, x, z)
    far_f = fetch_quarter(w_f[:half_f], x, z) + fetch_quarter(w_f[half_f:], x, z)

    qkv0, mixed_a0, lse_a0, part = self_forward(table_lengths, tokens, gain_a, w_a, heads)
    kv0, k0, v0 = memory_forward(memory, w_b, heads)
    qkv1, mixed_a1, lse_a1, part, w_a1 = self_forward(
        table_lengths, tokens, gain_a, None, heads, remote=(ctl,) + far_a + (part,)
    )
    kv1, k1, v1, w_b1 = memory_forward(memory, None, heads, remote=(ctl,) + far_b)
    q0, mixed_b0, lse_b0, part, first, normed_b = cross_forward(
        table_lengths, table_plots, w_b, kv0, k0, heads,
        lead=(tokens, part, swap(part, "mp", 1), gain_b),
    )
    q1, mixed_b1, lse_b1, part = cross_forward(
        table_lengths, table_plots, w_b1, kv1, k1, heads, follow=(normed_b, part)
    )
    res, back, second, normed_c, grad_f = feed(
        units, lead=(first, part, swap(part, "mp", 1), gain_c, cotangent, w_f)
    )
    res, back = feed(units, follow=(ctl, normed_c, cotangent, far_f, res, back))
    back_other = swap(back, "mp", 1)
    layer_out = (second + (res + swap(res, "mp", 1))).astype(BF16)

    grad_f = scatter_rows(grad_f)
    back, back_mem, grad_second, branch_b, gain_grad_c, grad_b = cross_backward(
        table_lengths, table_plots, w_b, q0, lse_b0, kv0, k0, v0, heads,
        lead=(second, back, back_other, cotangent, gain_c, normed_b, memory, mixed_b0),
    )
    back, back_mem = cross_backward(
        table_lengths, table_plots, w_b1, q1, lse_b1, kv1, k1, v1, heads,
        follow=(branch_b, back, back_mem),
    )
    back_other = swap(back, "mp", 1)
    grad_memory = back_mem + swap(back_mem, "mp", 1)
    grad_b = scatter_rows(grad_b)
    back, grad_first, branch_a, gain_grad_b, grad_a = self_backward(
        table_lengths, w_a, qkv0, lse_a0, heads,
        lead=(first, back, back_other, grad_second, gain_b, tokens, gain_a, mixed_a0),
    )
    grad_a = scatter_rows(grad_a)
    (back,) = self_backward(table_lengths, w_a1, qkv1, lse_a1, heads, follow=(branch_a, back))
    grad_tokens, gain_grad_a = tail(tokens, back, swap(back, "mp", 1), grad_first, gain_a)

    early = [
        grad_f[:, : 2 * units],
        grad_f[:, 2 * units :],
        grad_b[:, :hq],
        grad_b[:, hq : 3 * hq],
        grad_b[:, 3 * hq :],
    ]
    steps_early = adafactor(early, width)
    late = [grad_a[:, : 3 * hq], grad_a[:, 3 * hq :]]
    gain_parts = jnp.concatenate([gain_grad_a[0], gain_grad_b[0], gain_grad_c[0]])
    steps_late, gain_sum = adafactor(late, width, gain_parts)
    own_rows = grad_f.shape[0]
    grad_gains = lax.dynamic_slice_in_dim(gain_sum.reshape(3, width), place * own_rows, own_rows, axis=1).T

    def qkv_shape(g):
        return g.reshape(own_rows, 3, hq)

    def kv_shape(g):
        return g.reshape(own_rows, 2, hq)

    def gu_shape(g):
        return g.reshape(own_rows, 2, units)

    return (
        layer_out,
        grad_tokens,
        grad_memory,
        grad_gains,
        qkv_shape(late[0]),
        late[1],
        early[2],
        kv_shape(early[3]),
        early[4],
        gu_shape(early[0]),
        early[1],
        qkv_shape(steps_late[0]),
        steps_late[1],
        steps_early[2],
        kv_shape(steps_early[3]),
        steps_early[4],
        gu_shape(steps_early[0]),
        steps_early[1],
    )


def solution(mesh):
    split = P("dp", None)
    cols = P(None, "mp")
    cols3 = P(None, None, "mp")
    both = P("dp", "mp")
    both3 = P("dp", None, "mp")
    return jax.shard_map(
        on_device,
        mesh=mesh,
        in_specs=(
            split, split, split, split, split, P(),
            cols3, cols, cols, cols3, cols, cols3, cols,
        ),
        out_specs=(
            split, split, split, split,
            both3, both, both, both3, both, both3, both,
            both3, both, both, both3, both, both3, both,
        ),
        check_vma=False,
    )
```

time: 1120 us -> 476 us (0.42)
  waiting for transfers between devices: 809 us -> 187 us
  Pallas kernels: 0 us -> 166 us
  matrix products: 132 us -> 0 us
  blocking collectives: 41.6 us -> 0 us
  starting transfers between devices: 2.03 us -> 39.5 us
  other arithmetic: 69.3 us -> 32.9 us
  between operations: 19.4 us -> 6.45 us
    psum x5 -> x0, waiting for transfers between devices: 343 us -> none  [the longest x3 235 us: branch_total(): return lax.psum(partial_out, 'mp')]
    reduce_scatter x5 -> x0, waiting for transfers between devices: 284 us -> none  [the longest x1 75.6 us: on_device(): lax.psum_scatter(partials[6], 'dp', scatter_dimension=0, tiled=True)]
    ppermute x0 -> x38, waiting for transfers between devices: none -> 187 us  [swap(): return lax.ppermute(value, axis, [(i, i ^ bit) for i in range(count)])]
    unnamed x16 -> x0, waiting for transfers between devices: 182 us -> none
    pallas_call x0 -> x13, Pallas kernels: none -> 166 us  [run(): pl.pallas_call(kernel, grid=(grid,), in_specs=[s for _, s in ins], out_sp...]
    dot_general x31 -> x0, matrix products: 111 us -> none  [the longest x2 20.5 us: attend_backward(): jnp.einsum('qhd,khd->hqk', grad_mixed, values, preferred_element_type=jnp...]
    psum x2 -> x0, blocking collectives: 41.6 us -> none  [the longest x1 36 us: adafactor_sharded(): summed = lax.psum(col_local + mean_local, 'dp')]
    ppermute x0 -> x38, starting transfers between devices: none -> 39.5 us  [swap(): return lax.ppermute(value, axis, [(i, i ^ bit) for i in range(count)])]
  transfers between devices with their start and end apart: 13 -> 38, of which waited for: 13 -> 16; matrix products, arithmetic and copies ran while one was open for 12% -> 11% of each run, Pallas kernels for 0% -> 24%
where the time goes in v1:
time: 476 us; the launch traced here: 467 us
  waiting for transfers between devices  187 us (39%)
  Pallas kernels  166 us (35%)
  starting transfers between devices  39.5 us (8%)
  local copies, waits for them, and re-layouts  34.5 us (7%)
  other arithmetic  32.9 us (7%)
  between operations  6.45 us (1%)
    ppermute x38, waiting for transfers between devices, swap(): return lax.ppermute(value, axis, [(i, i ^ bit) for i in range(count)])  187 us
    pallas_call x13, Pallas kernels, run(): pl.pallas_call(kernel, grid=(grid,), in_specs=[s for _, s in ins], out_sp...  166 us
    ppermute x38, starting transfers between devices, swap(): return lax.ppermute(value, axis, [(i, i ^ bit) for i in range(count)])  39.5 us
    unnamed x95, local copies, waits for them, and re-layouts  10.3 us
  transfers between devices with their start and end apart: 38, of which 16 were waited for; matrix products, arithmetic and copies ran while one was open for 11% of the time, Pallas kernels for 24%

profile of v1, /device:TPU:0, one launch (start us, length us, event | category | flops | bytes accessed | tf_op | source)
XLA Modules:
  0.0 466.8 jit_solution(5990152596633135829)
XLA Ops:
  6.0 26.0 %collective-permute-done.refs_4_ = f32[384,768]{1,0:T(8,128)S(1)} collective-permute-done((f32[384,768]{1,0:T(8,128)S(1)}, f32[384,768]{1,0:T(8,128)S(1)}, u32[]{:S(2)}, u32[]{:S(2)}) %collective-permute-start) | collective-permute-done | bytes 1179680 | tf_op jit(solution)/shard_map/ppermute | solution.py:714
  37.8 11.4 %self_forward.2 = (bf16[576,1024]{1,0:T(8,128)(2,1)}, bf16[192,1024]{1,0:T(8,128)(2,1)}, f32[8,1024]{1,0:T(8,128)}, f32[1024,768]{1,0:T(8,128)}) custom-call(s32[1,4]{1,0:T(1,128)} %refs_0_.17, bf16[1024,768]{1,0:T(8,128)(2,1)} %tokens.1, f32[1,768]{1,0:T(1,128)} %get-tuple-element.205.refs_2_.refs_3_.refs_7_.gain, ...), custom_call_target="tpu_custom_call" | custom-call | flops 2013265920 | bytes 7506960 | tf_op jit(solution)/shard_map/self_forward/pallas_call | solution.py:116
  50.2 12.6 %self_forward.3 = (bf16[576,1024]{1,0:T(8,128)(2,1)}, bf16[192,1024]{1,0:T(8,128)(2,1)}, f32[8,1024]{1,0:T(8,128)}, f32[1024,768]{1,0:T(8,128)}, bf16[768,768]{1,0:T(8,128)(2,1)}) custom-call(s32[1,4]{1,0:T(1,128)} %refs_0_.17, s32[2]{0:T(128)} %pad_add_fusion.refs_1_.refs_0_, bf16[1024,768]{1,0:T(8,128)(2,1)} %tokens.1, ...), custom_call_target="tpu_custom_call" | custom-call | flops 2013265920 | bytes 13011992 | tf_op jit(solution)/shard_map/self_forward/pallas_call | solution.py:116
  64.5 26.8 %collective-permute-done.4.refs_2_ = f32[384,768]{1,0:T(8,128)S(1)} collective-permute-done((f32[384,768]{1,0:T(8,128)S(1)}, f32[384,768]{1,0:T(8,128)S(1)}, u32[]{:S(2)}, u32[]{:S(2)}) %collective-permute-start.4) | collective-permute-done | bytes 1179680 | tf_op jit(solution)/shard_map/ppermute | solution.py:714
  93.4 4.9 %memory_forward.2 = (bf16[384,1024]{1,0:T(8,128)(2,1)}, bf16[3,1024,64]{2,1,0:T(8,128)(2,1)}, bf16[3,1024,64]{2,1,0:T(8,128)(2,1)}) custom-call(bf16[1024,768]{1,0:T(8,128)(2,1)} %refs_8_.1, bf16[768,768]{1,0:T(8,128)(2,1)} %pad_maximum_fusion.2.refs_1_.refs_6_.refs_9_), custom_call_target="tpu_custom_call" | custom-call | flops 603979776 | bytes 4325376 | tf_op jit(solution)/shard_map/memory_forward/pallas_call | solution.py:116
  98.3 8.1 %collective-permute-done.6.refs_4_ = f32[192,768]{1,0:T(8,128)S(1)} collective-permute-done((f32[192,768]{1,0:T(8,128)S(1)}, f32[192,768]{1,0:T(8,128)S(1)}, u32[]{:S(2)}, u32[]{:S(2)}) %collective-permute-start.6) | collective-permute-done | bytes 589856 | tf_op jit(solution)/shard_map/ppermute | solution.py:714
  108.1 5.8 %memory_forward.3 = (bf16[384,1024]{1,0:T(8,128)(2,1)}, bf16[3,1024,64]{2,1,0:T(8,128)(2,1)}, bf16[3,1024,64]{2,1,0:T(8,128)(2,1)}, bf16[768,768]{1,0:T(8,128)(2,1)}) custom-call(s32[2]{0:T(128)} %pad_add_fusion.refs_1_.refs_0_, bf16[1024,768]{1,0:T(8,128)(2,1)} %refs_8_.1, f32[384,768]{1,0:T(8,128)} %copy-done.1, f32[192,768]{1,0:T(8,128)} %copy-done.23, ...), custom_call_target="tpu_custom_call" | custom-call | flops 603979776 | bytes 6684680 | tf_op jit(solution)/shard_map/memory_forward/pallas_call | solution.py:116
  115.6 12.7 %cross_forward.2 = (bf16[192,1024]{1,0:T(8,128)(2,1)}, bf16[192,1024]{1,0:T(8,128)(2,1)}, f32[8,1024]{1,0:T(8,128)}, f32[1024,768]{1,0:T(8,128)}, f32[1024,768]{1,0:T(8,128)}, /*index=5*/bf16[1024,768]{1,0:T(8,128)(2,1)}) custom-call(s32[1,4]{1,0:T(1,128)} %refs_0_.17, s32[1,4]{1,0:T(1,128)} %refs_1_.11, bf16[1024,768]{1,0:T(8,128)(2,1)} %tokens.1, ...), custom_call_target="tpu_custom_call" | custom-call | flops 1006632960 | bytes 18910240 | tf_op jit(solution)/shard_map/cross_forward/pallas_call | solution.py:116
  128.2 11.0 %cross_forward.3 = (bf16[192,1024]{1,0:T(8,128)(2,1)}, bf16[192,1024]{1,0:T(8,128)(2,1)}, f32[8,1024]{1,0:T(8,128)}, f32[1024,768]{1,0:T(8,128)}) custom-call(s32[1,4]{1,0:T(1,128)} %refs_0_.17, s32[1,4]{1,0:T(1,128)} %refs_1_.11, bf16[1024,768]{1,0:T(8,128)(2,1)} %get-tuple-element.69.refs_2_.refs_7_, bf16[768,768]{1,0:T(8,128)(2,1)} %get-tuple-element.70.refs_3_, ...), custom_call_target="tpu_custom_call" | custom-call | flops 1006632960 | bytes 11042848 | tf_op jit(solution)/shard_map/cross_forward/pallas_call | solution.py:116
  147.4 25.1 %collective-permute-done.8.refs_3_ = f32[384,768]{1,0:T(8,128)S(1)} collective-permute-done((f32[384,768]{1,0:T(8,128)S(1)}, f32[384,768]{1,0:T(8,128)S(1)}, u32[]{:S(2)}, u32[]{:S(2)}) %collective-permute-start.8) | collective-permute-done | bytes 1179680 | tf_op jit(solution)/shard_map/ppermute | solution.py:714
  175.9 21.5 %collective-permute-done.11.refs_6_ = f32[384,768]{1,0:T(8,128)S(1)} collective-permute-done((f32[384,768]{1,0:T(8,128)S(1)}, f32[384,768]{1,0:T(8,128)S(1)}, u32[]{:S(2)}, u32[]{:S(2)}) %collective-permute-start.11) | collective-permute-done | bytes 1179680 | tf_op jit(solution)/shard_map/ppermute | solution.py:714
  200.7 16.0 %feed.2 = (f32[1024,768]{1,0:T(8,128)}, f32[1024,768]{1,0:T(8,128)}, f32[1024,768]{1,0:T(8,128)}, bf16[1024,768]{1,0:T(8,128)(2,1)}, f32[768,1536]{1,0:T(8,128)}) custom-call(f32[1024,768]{1,0:T(8,128)} %get-tuple-element.68.refs_0_.refs_1_, f32[1024,768]{1,0:T(8,128)} %get-tuple-element.74.refs_1_, f32[1024,768]{1,0:T(8,128)} %collective-permute-done.7.refs_2_, ...), custom_call_target="tpu_custom_call" | custom-call | flops 7247757312 | bytes 29101056 | tf_op jit(solution)/shard_map/feed/pallas_call | solution.py:116
  218.3 11.4 %feed.3 = (f32[1024,768]{1,0:T(8,128)}, f32[1024,768]{1,0:T(8,128)}) custom-call(s32[2]{0:T(128)} %pad_add_fusion.refs_1_.refs_0_, bf16[1024,768]{1,0:T(8,128)(2,1)} %get-tuple-element.76.refs_1_, bf16[1024,768]{1,0:T(8,128)(2,1)} %refs_5_.1, f32[384,768]{1,0:T(8,128)} %copy-done.17, f32[192,768]{1,0:T(8,128)} %copy-done.39, f32[192,768]{1,0:T(8,128)} %copy-done.38, ...), custom_call_target="tpu_custom_call" | custom-call | flops 4831838208 | bytes 20447240 | tf_op jit(solution)/shard_map/feed/pallas_call | solution.py:116
  237.3 20.9 %cross_backward.2 = (f32[1024,768]{1,0:T(8,128)}, f32[1024,768]{1,0:T(8,128)}, f32[1024,768]{1,0:T(8,128)}, bf16[1024,768]{1,0:T(8,128)(2,1)}, f32[8,768]{1,0:T(8,128)}, /*index=5*/f32[768,768]{1,0:T(8,128)}) custom-call(s32[1,4]{1,0:T(1,128)} %refs_0_.17, s32[1,4]{1,0:T(1,128)} %refs_1_.11, f32[1024,768]{1,0:T(8,128)} %get-tuple-element.75.refs_2_, ...), custom_call_target="tpu_custom_call" | custom-call | flops 3422552064 | bytes 31124512 | tf_op jit(solution)/shard_map/cross_backward/pallas_call | solution.py:116
  258.2 16.5 %cross_backward.3 = (f32[1024,768]{1,0:T(8,128)}, f32[1024,768]{1,0:T(8,128)}) custom-call(s32[1,4]{1,0:T(1,128)} %refs_0_.17, s32[1,4]{1,0:T(1,128)} %refs_1_.11, bf16[1024,768]{1,0:T(8,128)(2,1)} %get-tuple-element.85.refs_2_, bf16[768,768]{1,0:T(8,128)(2,1)} %get-tuple-element.70.refs_3_, bf16[192,1024]{1,0:T(8,128)(2,1)} %get-tuple-element.86.refs_4_, ...), custom_call_target="tpu_custom_call" | custom-call | flops 2214592512 | bytes 17334304 | tf_op jit(solution)/shard_map/cross_backward/pallas_call | solution.py:116
  274.9 12.0 %collective-permute-done.30 = f32[4,96,1536]{2,1,0:T(8,128)} collective-permute-done((f32[4,96,1536]{2,1,0:T(8,128)}, f32[4,96,1536]{2,1,0:T(8,128)}, u32[]{:S(2)}, u32[]{:S(2)}) %collective-permute-start.30) | collective-permute-done | bytes 2359328 | tf_op jit(solution)/shard_map/ppermute | solution.py:714
  293.3 24.7 %collective-permute-done.31 = f32[2,96,1536]{2,1,0:T(8,128)} collective-permute-done((f32[2,96,1536]{2,1,0:T(8,128)}, f32[2,96,1536]{2,1,0:T(8,128)}, u32[]{:S(2)}, u32[]{:S(2)}) %collective-permute-start.31) | collective-permute-done | bytes 1179680 | tf_op jit(solution)/shard_map/ppermute | solution.py:714
  324.8 20.8 %self_backward.2 = (f32[1024,768]{1,0:T(8,128)}, f32[1024,768]{1,0:T(8,128)}, bf16[1024,768]{1,0:T(8,128)(2,1)}, f32[8,768]{1,0:T(8,128)}, f32[768,768]{1,0:T(8,128)}) custom-call(s32[1,4]{1,0:T(1,128)} %refs_0_.17, f32[1024,768]{1,0:T(8,128)} %get-tuple-element.68.refs_0_.refs_1_, f32[1024,768]{1,0:T(8,128)} %get-tuple-element.91.refs_2_, ...), custom_call_target="tpu_custom_call" | custom-call | flops 4429185024 | bytes 27195408 | tf_op jit(solution)/shard_map/self_backward/pallas_call | solution.py:116
  350.8 22.6 %collective-permute-done.19 = f32[4,96,768]{2,1,0:T(8,128)S(1)} collective-permute-done((f32[4,96,768]{2,1,0:T(8,128)S(1)}, f32[4,96,768]{2,1,0:T(8,128)S(1)}, u32[]{:S(2)}, u32[]{:S(2)}) %collective-permute-start.19) | collective-permute-done | bytes 1179680 | tf_op jit(solution)/shard_map/ppermute | solution.py:714
  376.5 9.9 %collective-permute-done.20 = f32[2,96,768]{2,1,0:T(8,128)S(1)} collective-permute-done((f32[2,96,768]{2,1,0:T(8,128)S(1)}, f32[2,96,768]{2,1,0:T(8,128)S(1)}, u32[]{:S(2)}, u32[]{:S(2)}) %collective-permute-start.20) | collective-permute-done | bytes 589856 | tf_op jit(solution)/shard_map/ppermute | solution.py:714
  387.2 15.3 %self_backward.3.part = f32[1024,768]{1,0:T(8,128)} custom-call(s32[1,4]{1,0:T(1,128)} %refs_0_.17, bf16[1024,768]{1,0:T(8,128)(2,1)} %get-tuple-element.96.refs_1_, bf16[768,768]{1,0:T(8,128)(2,1)} %get-tuple-element.97.refs_2_, bf16[576,1024]{1,0:T(8,128)(2,1)} %get-tuple-element.98.refs_3_, f32[8,1024]{1,0:T(8,128)} %get-tuple-element.99.refs_4_, ...), custom_call_target="tpu_custom_call" | custom-call | flops 3221225472 | bytes 10256400 | tf_op jit(solution)/shard_map/self_backward/pallas_call | solution.py:116
  419.4 4.6 add_convert_fusion
  431.1 4.3 add.236
  439.2 6.9 %last_norm.1 = (f32[1024,768]{1,0:T(8,128)}, f32[8,768]{1,0:T(8,128)}) custom-call(bf16[1024,768]{1,0:T(8,128)(2,1)} %tokens.1, f32[1024,768]{1,0:T(8,128)} %self_backward.3.part, f32[1024,768]{1,0:T(8,128)} %collective-permute-done.17.other, f32[1024,768]{1,0:T(8,128)} %get-tuple-element.101.carried, f32[1,768]{1,0:T(1,128)} %get-tuple-element.205.refs_2_.refs_3_.refs_7_.gain), custom_call_target="tpu_custom_call" | custom-call | flops 15728640 | bytes 14183424 | tf_op jit(solution)/shard_map/last_norm/pallas_call | solution.py:116
  (247 shorter events, 108.7 us)
Async XLA Ops:
  3.0 29.0 %collective-permute-start = (f32[384,768]{1,0:T(8,128)S(1)}, f32[384,768]{1,0:T(8,128)S(1)}, u32[]{:S(2)}, u32[]{:S(2)}) collective-permute-start(f32[384,768]{1,0:T(8,128)S(1)} %maximum_convert_fusion), channel_id=1, source_target_pairs={{0,2},{1,3},{2,0},{3,1},{4,6},{5,7},{6,4},{7,5},{8,10},{9,11},{10,... | collective-permute-start | bytes 3538952 | tf_op jit(solution)/shard_map/ppermute | solution.py:714
  32.1 17.1 %collective-permute-start.2 = (f32[192,768]{1,0:T(8,128)S(1)}, f32[192,768]{1,0:T(8,128)S(1)}, u32[]{:S(2)}, u32[]{:S(2)}) collective-permute-start(f32[192,768]{1,0:T(8,128)S(1)} %get-tuple-element.180), channel_id=1, source_target_pairs={{0,8},{4,12},{8,0},{12,4},{16,24},{20,28},{24,16},{28,20},{1,9},{5... | collective-permute-start | bytes 1769480 | tf_op jit(solution)/shard_map/ppermute | solution.py:714
  62.7 51.1 %collective-permute-start.3 = (f32[1024,768]{1,0:T(8,128)}, f32[1024,768]{1,0:T(8,128)S(1)}, u32[]{:S(2)}, u32[]{:S(2)}) collective-permute-start(f32[1024,768]{1,0:T(8,128)} %get-tuple-element.65.refs_3_), channel_id=1, source_target_pairs={{0,1},{1,0},{2,3},{3,2},{4,5},{5,4},{6,7},{7,6},{8,9},{9,8},{10,11... | collective-permute-start | bytes 9437192 | tf_op jit(solution)/shard_map/ppermute | solution.py:714
  62.9 28.4 %collective-permute-start.4 = (f32[384,768]{1,0:T(8,128)S(1)}, f32[384,768]{1,0:T(8,128)S(1)}, u32[]{:S(2)}, u32[]{:S(2)}) collective-permute-start(f32[384,768]{1,0:T(8,128)S(1)} %maximum_convert_fusion.1), channel_id=1, source_target_pairs={{0,2},{1,3},{2,0},{3,1},{4,6},{5,7},{6,4},{7,5},{8,10},{9,11},{10,... | collective-permute-start | bytes 3538952 | tf_op jit(solution)/shard_map/ppermute | solution.py:714
  139.3 61.5 %collective-permute-start.7 = (f32[1024,768]{1,0:T(8,128)}, f32[1024,768]{1,0:T(8,128)}, u32[]{:S(2)}, u32[]{:S(2)}) collective-permute-start(f32[1024,768]{1,0:T(8,128)} %get-tuple-element.74.refs_1_), channel_id=1, source_target_pairs={{0,1},{1,0},{2,3},{3,2},{4,5},{5,4},{6,7},{7,6},{8,9},{9,8},{10,11... | collective-permute-start | bytes 9437192 | tf_op jit(solution)/shard_map/ppermute | solution.py:714
  143.7 28.8 %collective-permute-start.8 = (f32[384,768]{1,0:T(8,128)S(1)}, f32[384,768]{1,0:T(8,128)S(1)}, u32[]{:S(2)}, u32[]{:S(2)}) collective-permute-start(f32[384,768]{1,0:T(8,128)S(1)} %maximum_convert_fusion.2), channel_id=1, source_target_pairs={{0,2},{1,3},{2,0},{3,1},{4,6},{5,7},{6,4},{7,5},{8,10},{9,11},{10,... | collective-permute-start | bytes 3538952 | tf_op jit(solution)/shard_map/ppermute | solution.py:714
  145.3 52.0 %collective-permute-start.11 = (f32[384,768]{1,0:T(8,128)S(1)}, f32[384,768]{1,0:T(8,128)S(1)}, u32[]{:S(2)}, u32[]{:S(2)}) collective-permute-start(f32[384,768]{1,0:T(8,128)S(1)} %maximum_convert_fusion.3), channel_id=1, source_target_pairs={{0,2},{1,3},{2,0},{3,1},{4,6},{5,7},{6,4},{7,5},{8,10},{9,11},{10,... | collective-permute-start | bytes 3538952 | tf_op jit(solution)/shard_map/ppermute | solution.py:714
  172.6 44.2 %collective-permute-start.10 = (f32[192,768]{1,0:T(8,128)S(1)}, f32[192,768]{1,0:T(8,128)S(1)}, u32[]{:S(2)}, u32[]{:S(2)}) collective-permute-start(f32[192,768]{1,0:T(8,128)S(1)} %get-tuple-element.176), channel_id=1, source_target_pairs={{0,8},{4,12},{8,0},{12,4},{16,24},{20,28},{24,16},{28,20},{1,9},{5... | collective-permute-start | bytes 1769480 | tf_op jit(solution)/shard_map/ppermute | solution.py:714
  175.3 41.5 %collective-permute-start.9 = (f32[192,768]{1,0:T(8,128)S(1)}, f32[192,768]{1,0:T(8,128)S(1)}, u32[]{:S(2)}, u32[]{:S(2)}) collective-permute-start(f32[192,768]{1,0:T(8,128)S(1)} %get-tuple-element.177), channel_id=1, source_target_pairs={{0,4},{4,0},{8,12},{12,8},{16,20},{20,16},{24,28},{28,24},{1,5},{5... | collective-permute-start | bytes 1769480 | tf_op jit(solution)/shard_map/ppermute | solution.py:714
  197.5 19.4 %collective-permute-start.13 = (f32[192,768]{1,0:T(8,128)S(1)}, f32[192,768]{1,0:T(8,128)S(1)}, u32[]{:S(2)}, u32[]{:S(2)}) collective-permute-start(f32[192,768]{1,0:T(8,128)S(1)} %get-tuple-element.174), channel_id=1, source_target_pairs={{0,8},{4,12},{8,0},{12,4},{16,24},{20,28},{24,16},{28,20},{1,9},{5... | collective-permute-start | bytes 1769480 | tf_op jit(solution)/shard_map/ppermute | solution.py:714
  200.2 16.6 %collective-permute-start.12 = (f32[192,768]{1,0:T(8,128)S(1)}, f32[192,768]{1,0:T(8,128)S(1)}, u32[]{:S(2)}, u32[]{:S(2)}) collective-permute-start(f32[192,768]{1,0:T(8,128)S(1)} %get-tuple-element.175), channel_id=1, source_target_pairs={{0,4},{4,0},{8,12},{12,8},{16,20},{20,16},{24,28},{28,24},{1,5},{5... | collective-permute-start | bytes 1769480 | tf_op jit(solution)/shard_map/ppermute | solution.py:714
  233.0 53.9 %collective-permute-start.30 = (f32[4,96,1536]{2,1,0:T(8,128)}, f32[4,96,1536]{2,1,0:T(8,128)}, u32[]{:S(2)}, u32[]{:S(2)}) collective-permute-start(f32[4,96,1536]{2,1,0:T(8,128)} %dynamic-slice_bitcast_fusion), channel_id=1, source_target_pairs={{0,4},{4,0},{8,12},{12,8},{16,20},{20,16},{24,28},{28,24},{1,5},{5... | collective-permute-start | bytes 7077896 | tf_op jit(solution)/shard_map/ppermute | solution.py:714
  274.7 50.0 %collective-permute-start.16 = (f32[1024,768]{1,0:T(8,128)}, f32[1024,768]{1,0:T(8,128)}, u32[]{:S(2)}, u32[]{:S(2)}) collective-permute-start(f32[1024,768]{1,0:T(8,128)} %get-tuple-element.91.refs_2_), channel_id=1, source_target_pairs={{0,1},{1,0},{2,3},{3,2},{4,5},{5,4},{6,7},{7,6},{8,9},{9,8},{10,11... | collective-permute-start | bytes 9437192 | tf_op jit(solution)/shard_map/ppermute | solution.py:714
  290.1 27.9 %collective-permute-start.31 = (f32[2,96,1536]{2,1,0:T(8,128)}, f32[2,96,1536]{2,1,0:T(8,128)}, u32[]{:S(2)}, u32[]{:S(2)}) collective-permute-start(f32[2,96,1536]{2,1,0:T(8,128)} %dynamic-slice_bitcast_fusion.1), channel_id=1, source_target_pairs={{0,8},{4,12},{8,0},{12,4},{16,24},{20,28},{24,16},{28,20},{1,9},{5... | collective-permute-start | bytes 3538952 | tf_op jit(solution)/shard_map/ppermute | solution.py:714
  291.2 31.0 %collective-permute-start.27 = (f32[4,96,768]{2,1,0:T(8,128)S(1)}, f32[4,96,768]{2,1,0:T(8,128)}, u32[]{:S(2)}, u32[]{:S(2)}) collective-permute-start(f32[4,96,768]{2,1,0:T(8,128)S(1)} %dynamic-slice_bitcast_fusion.2), channel_id=1, source_target_pairs={{0,4},{4,0},{8,12},{12,8},{16,20},{20,16},{24,28},{28,24},{1,5},{5... | collective-permute-start | bytes 3538952 | tf_op jit(solution)/shard_map/ppermute | solution.py:714
  292.8 126.7 %collective-permute-start.14 = (f32[1024,768]{1,0:T(8,128)}, f32[1024,768]{1,0:T(8,128)}, u32[]{:S(2)}, u32[]{:S(2)}) collective-permute-start(f32[1024,768]{1,0:T(8,128)} %get-tuple-element.79), channel_id=1, source_target_pairs={{0,1},{1,0},{2,3},{3,2},{4,5},{5,4},{6,7},{7,6},{8,9},{9,8},{10,11... | collective-permute-start | bytes 9437192 | tf_op jit(solution)/shard_map/ppermute | solution.py:714
  292.8 138.3 %collective-permute-start.18 = (f32[1024,768]{1,0:T(8,128)}, f32[1024,768]{1,0:T(8,128)}, u32[]{:S(2)}, u32[]{:S(2)}) collective-permute-start(f32[1024,768]{1,0:T(8,128)} %get-tuple-element.103), channel_id=1, source_target_pairs={{0,1},{1,0},{2,3},{3,2},{4,5},{5,4},{6,7},{7,6},{8,9},{9,8},{10,11... | collective-permute-start | bytes 9437192 | tf_op jit(solution)/shard_map/ppermute | solution.py:714
  319.4 29.1 %collective-permute-start.32 = (f32[1,96,1536]{2,1,0:T(8,128)S(1)}, f32[1,96,1536]{2,1,0:T(8,128)S(1)}, u32[]{:S(2)}, u32[]{:S(2)}) collective-permute-start(f32[1,96,1536]{2,1,0:T(8,128)S(1)} %constant_dynamic-slice_fusion), channel_id=1, source_target_pairs={{0,16},{4,20},{8,24},{12,28},{16,0},{20,4},{24,8},{28,12},{1,17},{... | collective-permute-start | bytes 1769480 | tf_op jit(solution)/shard_map/ppermute | solution.py:714
  323.6 26.9 %collective-permute-start.28 = (f32[2,96,768]{2,1,0:T(8,128)S(1)}, f32[2,96,768]{2,1,0:T(8,128)S(1)}, u32[]{:S(2)}, u32[]{:S(2)}) collective-permute-start(f32[2,96,768]{2,1,0:T(8,128)S(1)} %dynamic-slice_bitcast_fusion.4), channel_id=1, source_target_pairs={{0,8},{4,12},{8,0},{12,4},{16,24},{20,28},{24,16},{28,20},{1,9},{5... | collective-permute-start | bytes 1769480 | tf_op jit(solution)/shard_map/ppermute | solution.py:714
  346.9 26.4 %collective-permute-start.19 = (f32[4,96,768]{2,1,0:T(8,128)S(1)}, f32[4,96,768]{2,1,0:T(8,128)S(1)}, u32[]{:S(2)}, u32[]{:S(2)}) collective-permute-start(f32[4,96,768]{2,1,0:T(8,128)S(1)} %dynamic-slice_bitcast_fusion.3), channel_id=1, source_target_pairs={{0,4},{4,0},{8,12},{12,8},{16,20},{20,16},{24,28},{28,24},{1,5},{5... | collective-permute-start | bytes 3538952 | tf_op jit(solution)/shard_map/ppermute | solution.py:714
  350.7 23.7 %collective-permute-start.29 = (f32[1,96,768]{2,1,0:T(8,128)S(1)}, f32[1,96,768]{2,1,0:T(8,128)S(1)}, u32[]{:S(2)}, u32[]{:S(2)}) collective-permute-start(f32[1,96,768]{2,1,0:T(8,128)S(1)} %constant_dynamic-slice_fusion.1), channel_id=1, source_target_pairs={{0,16},{4,20},{8,24},{12,28},{16,0},{20,4},{24,8},{28,12},{1,17},{... | collective-permute-start | bytes 884744 | tf_op jit(solution)/shard_map/ppermute | solution.py:714
  376.4 27.5 %collective-permute-start.33 = (f32[5,96]{1,0:T(8,128)S(1)}, f32[5,96]{1,0:T(8,128)S(1)}, u32[]{:S(2)}, u32[]{:S(2)}) collective-permute-start(f32[5,96]{1,0:T(8,128)S(1)} %stack.70), channel_id=1, source_target_pairs={{0,1},{1,0},{2,3},{3,2},{4,5},{5,4},{6,7},{7,6},{8,9},{9,8},{10,11... | collective-permute-start | bytes 5768 | tf_op jit(solution)/shard_map/ppermute | solution.py:714
  386.5 16.0 %collective-permute-start.21 = (f32[1,96,768]{2,1,0:T(8,128)S(1)}, f32[1,96,768]{2,1,0:T(8,128)S(1)}, u32[]{:S(2)}, u32[]{:S(2)}) collective-permute-start(f32[1,96,768]{2,1,0:T(8,128)S(1)} %constant_dynamic-slice_fusion.3), channel_id=1, source_target_pairs={{0,16},{4,20},{8,24},{12,28},{16,0},{20,4},{24,8},{28,12},{1,17},{... | collective-permute-start | bytes 884744 | tf_op jit(solution)/shard_map/ppermute | solution.py:714
  402.5 36.6 %collective-permute-start.17 = (f32[1024,768]{1,0:T(8,128)}, f32[1024,768]{1,0:T(8,128)}, u32[]{:S(2)}, u32[]{:S(2)}) collective-permute-start(f32[1024,768]{1,0:T(8,128)} %self_backward.3.part), channel_id=1, source_target_pairs={{0,1},{1,0},{2,3},{3,2},{4,5},{5,4},{6,7},{7,6},{8,9},{9,8},{10,11... | collective-permute-start | bytes 9437192 | tf_op jit(solution)/shard_map/ppermute | solution.py:714
  (60 other events, 656.3 us)
